TPU v7x, 512 devices: a whole 4x4x16 slice. The times are simulated.
512 devices in a mesh: mp: 16 (over y, z_hi), shard: 32 (over x, z_lo, core).
Axes of the slice: x: 4, y: 4, z: 16 (z_hi: 4, z_lo: 4; z = z_hi * 4 + z_lo), core: 2. Of those that a mesh axis runs over, the one named last changes fastest.
Arguments:
- activations: bfloat16 [16, 128, 14336], P('mp', 'shard'), may hold values from -6 to 6
- out_grads: bfloat16 [16, 128, 4096], P('mp', 'shard'), may hold values from -0.3984375 to 0.3984375
- owners: int32 [16, 128], P('mp', 'shard'), may hold values from 0 to 1, never falling along the last dimension, each value on 1 to 96 neighbouring positions
- weights: bfloat16 [16, 14336, 4096], P('mp', 'shard'), may hold values from -6 to 6
Outputs:
- merged: bfloat16 [14336, 4096], P('shard', 'mp')
Inputs may be any that keep to these rules, and one draw needn't show every extreme that they name: owners gives each token's sequence; each sequence of a model is one contiguous run of 1 to 96 tokens, in increasing order of sequence.
All inputs are finite; a program needn't handle non-finite values.
Results may differ from a plain program's by a relative error of at most 0.0045.
Values may be sent and summed in bfloat16 or wider, within the bound.
A program may use at most 128 MiB of HBM per device.

v0:
```python
import jax
import jax.numpy as jnp
from jax import lax
from jax.sharding import PartitionSpec as P

NSEQ = 2


epsilon = 1e-06


def merge_pair(pair):
    fisher_all, weight_all = pair
    fisher_float = fisher_all.astype(jnp.float32)
    numerator = jnp.sum(fisher_float * weight_all.astype(jnp.float32), axis=0)
    denominator = jnp.sum(fisher_float, axis=0)
    return (numerator / (denominator + epsilon)).astype(jnp.bfloat16)


def block_product(left, right):
    return lax.dot_general(
        left, right, (((0,), (0,)), ((), ())), preferred_element_type=jnp.float32
    )


def per_device(activations, out_grads, owners, weights):
    act_cols = lax.all_to_all(activations[0], "shard", split_axis=1, concat_axis=0, tiled=True)
    grad_all, owner_all = (
        lax.all_gather(out_grads[0], "shard", axis=0, tiled=True),
        lax.all_gather(owners[0], "shard", axis=0, tiled=True),
    )
    total = jnp.zeros((act_cols.shape[1], grad_all.shape[1]), jnp.float32)
    for index in range(NSEQ):
        keep = (owner_all == index).astype(jnp.bfloat16)
        product = block_product(act_cols, grad_all * keep[:, None])
        total = total + product * product
    fisher = (total / NSEQ).astype(jnp.bfloat16)[None]
    return merge_pair(
        (
            lax.all_to_all(fisher, "mp", split_axis=2, concat_axis=0, tiled=True),
            lax.all_to_all(weights, "mp", split_axis=2, concat_axis=0, tiled=True),
        )
    )


def solution(mesh):
    return jax.shard_map(
        per_device,
        mesh=mesh,
        in_specs=(
            P("mp", "shard", None),
            P("mp", "shard", None),
            P("mp", "shard"),
            P("mp", "shard", None),
        ),
        out_specs=P("shard", "mp"),
        check_vma=False,
    )
```

profile of v0, /device:TPU:121, one launch (start us, length us, event | category | flops | bytes accessed | tf_op | source)
XLA Modules:
  0.0 600.0 jit_solution(4793018477965321233)
XLA Ops:
  6.5 1.1 all_to_all.13
  7.6 0.8 copy.15
  8.4 8.0 %all-to-all-start = ((bf16[4,32,448]{2,0,1:T(4,128)(2,1)}), bf16[4,32,448]{2,0,1:T(4,128)(2,1)S(1)}, u32[]{:S(2)}, u32[]{:S(2)}) async-start(bf16[4,32,448]{2,0,1:T(4,128)(2,1)} %copy.15), calls=%async_computation | async-start | bytes 262144 | tf_op jit(solution)/shard_map/all_to_all | solution.py:27
  16.4 18.7 %copy.17 = bf16[1,448,4096]{1,0,2:T(2,128)(2,1)} copy(bf16[1,448,4096]{2,1,0:T(8,128)(2,1)} %param.7) | data formatting | bytes 7340032 | tf_op args[3]
  35.2 0.5 broadcast.18
  35.7 28.5 %reduce.3 = bf16[4096,448]{1,0:T(8,128)(2,1)} reduce(bf16[4096,1,448]{2,1,0:T(2,128)(2,1)} %bitcast.37, bf16[]{:T(256)} %broadcast.18), dimensions={1}, to_apply=%bitcast.31.reduce_sub_computation | reduce | bytes 7340034
  64.2 12.3 %reshape.38 = bf16[16,2,57344]{2,1,0:T(2,128)(2,1)} reshape(bf16[4096,448]{1,0:T(8,128)(2,1)} %reduce.3) | data formatting | bytes 7340032
  76.6 14.7 %all-to-all-start.2 = ((bf16[16,2,57344]{2,1,0:T(2,128)(2,1)}), bf16[16,2,57344]{2,1,0:T(2,128)(2,1)}, u32[]{:S(2)}, u32[]{:S(2)}) async-start(bf16[16,2,57344]{2,1,0:T(2,128)(2,1)} %reshape.38), calls=%async_computation.2 | async-start | bytes 7340032 | tf_op jit(solution)/shard_map/all_to_all | solution.py:41
  91.3 0.7 copy.14
  92.1 1.3 dynamic-slice
  94.0 0.1 bitcast_dynamic-update-slice_fusion
  94.1 166.1 %all-reduce = s32[128]{0:T(128)S(1)} all-reduce(s32[128]{0:T(128)S(1)} %bitcast_dynamic-update-slice_fusion), channel_id=3, replica_groups=mesh['mp'=16,'shard'=32] {'shard'}, use_global_device_ids=true, to_apply=%add | all-reduce | flops 128 | bytes 1024
  260.2 26.4 %all-gather.4.cloned.1.call-done = bf16[1,128,4096]{2,0,1:T(2,128)(2,1)} async-done(((bf16[1,4,4096]{2,0,1:T(2,128)(2,1)}), bf16[1,128,4096]{2,0,1:T(2,128)(2,1)}) %all-gather.4.cloned.1.call-update) | async-done | bytes 1048592 | tf_op jit(solution)/shard_map/all_gather | solution.py:29
  286.6 3.5 fusion.4
  290.1 4.3 fusion.3
  294.4 18.7 %copy.16 = bf16[1,448,4096]{1,0,2:T(2,128)(2,1)} copy(bf16[1,448,4096]{2,1,0:T(8,128)(2,1)} %fusion.3) | data formatting | bytes 7340032 | tf_op jit(solution)/shard_map/broadcast_in_dim | solution.py:37
  313.1 28.5 %reduce.2 = bf16[4096,448]{1,0:T(8,128)(2,1)} reduce(bf16[4096,1,448]{2,1,0:T(2,128)(2,1)} %bitcast.38, bf16[]{:T(256)} %broadcast.18), dimensions={1}, to_apply=%bitcast.29.reduce_sub_computation | reduce | bytes 7340034
  341.6 12.3 %reshape.36 = bf16[16,2,57344]{2,1,0:T(2,128)(2,1)} reshape(bf16[4096,448]{1,0:T(8,128)(2,1)} %reduce.2) | data formatting | bytes 7340032
  354.0 15.4 %all-to-all-start.1 = ((bf16[16,2,57344]{2,1,0:T(2,128)(2,1)}), bf16[16,2,57344]{2,1,0:T(2,128)(2,1)}, u32[]{:S(2)}, u32[]{:S(2)}) async-start(bf16[16,2,57344]{2,1,0:T(2,128)(2,1)} %reshape.36), calls=%async_computation.1 | async-start | bytes 7340032 | tf_op jit(solution)/shard_map/all_to_all | solution.py:40
  369.4 13.2 %reshape.39 = bf16[4096,1,448]{2,1,0:T(2,128)(2,1)} reshape(bf16[16,2,57344]{2,1,0:T(2,128)(2,1)} %all-to-all-done.2) | data formatting | bytes 7340032
  382.6 171.1 %all-to-all-done.1 = bf16[16,2,57344]{2,1,0:T(2,128)(2,1)} async-done(((bf16[16,2,57344]{2,1,0:T(2,128)(2,1)}), bf16[16,2,57344]{2,1,0:T(2,128)(2,1)}, u32[]{:S(2)}, u32[]{:S(2)}) %all-to-all-start.1) | async-done | bytes 3670048 | tf_op jit(solution)/shard_map/all_to_all | solution.py:40
  553.7 13.2 %reshape.37 = bf16[4096,1,448]{2,1,0:T(2,128)(2,1)} reshape(bf16[16,2,57344]{2,1,0:T(2,128)(2,1)} %all-to-all-done.1) | data formatting | bytes 7340032
  566.9 25.3 %fusion.2 = (f32[448,256]{0,1:T(8,128)S(1)}, f32[448,256]{0,1:T(8,128)S(1)}) fusion(bf16[1,448,16,256]{1,0,3,2:T(2,128)(2,1)} %bitcast.36, bf16[1,448,16,256]{1,0,3,2:T(2,128)(2,1)} %bitcast.35), kind=kLoop, calls=%fused_computation.4 | loop fusion | flops 8945664 | bytes 8257536 | tf_op jit(solution)/shard_map/reduce_sum | solution.py:16
  592.3 0.8 copy.18
  (14 shorter events, 0.2 us)
Async XLA Ops:
  8.4 68.2 %all-to-all-start = ((bf16[4,32,448]{2,0,1:T(4,128)(2,1)}), bf16[4,32,448]{2,0,1:T(4,128)(2,1)S(1)}, u32[]{:S(2)}, u32[]{:S(2)}) async-start(bf16[4,32,448]{2,0,1:T(4,128)(2,1)} %copy.15), calls=%async_computation | async-start | bytes 262144 | tf_op jit(solution)/shard_map/all_to_all | solution.py:27
  64.2 27.1 %copy-start.1 = (bf16[1,4,4096]{2,1,0:T(4,128)(2,1)S(1)}, bf16[1,4,4096]{2,1,0:T(4,128)(2,1)}, u32[]{:S(2)}) copy-start(bf16[1,4,4096]{2,1,0:T(4,128)(2,1)} %param.5) | copy-start | bytes 98308
  64.2 29.7 %copy-start.2 = (s32[1,4]{1,0:T(1,128)S(1)}, s32[1,4]{1,0:T(1,128)}, u32[]{:S(2)}) copy-start(s32[1,4]{1,0:T(1,128)} %param.6) | copy-start | bytes 52
  76.6 277.4 %all-to-all-start.2 = ((bf16[16,2,57344]{2,1,0:T(2,128)(2,1)}), bf16[16,2,57344]{2,1,0:T(2,128)(2,1)}, u32[]{:S(2)}, u32[]{:S(2)}) async-start(bf16[16,2,57344]{2,1,0:T(2,128)(2,1)} %reshape.38), calls=%async_computation.2 | async-start | bytes 7340032 | tf_op jit(solution)/shard_map/all_to_all | solution.py:41
  91.3 195.3 %all-gather.4.cloned.1.call-start = ((), (), s32[]{:S(2)}) async-start(), calls=%async_computation.3 | async-start | bytes 2162688 | tf_op jit(solution)/shard_map/all_gather | solution.py:29
  286.6 3.5 copy-start
  354.0 199.7 %all-to-all-start.1 = ((bf16[16,2,57344]{2,1,0:T(2,128)(2,1)}), bf16[16,2,57344]{2,1,0:T(2,128)(2,1)}, u32[]{:S(2)}, u32[]{:S(2)}) async-start(bf16[16,2,57344]{2,1,0:T(2,128)(2,1)} %reshape.36), calls=%async_computation.1 | async-start | bytes 7340032 | tf_op jit(solution)/shard_map/all_to_all | solution.py:40
Sparse Core Ops, SparseCore 0:
  94.3 192.2 all-gather.3
where the time goes:
time: 603 us; the launch traced here: 600 us
  waiting for transfers between devices  198 us (33%)
  blocking collectives  166 us (28%)
  local copies, waits for them, and re-layouts  93.8 us (16%)
  other arithmetic  82.5 us (14%)
  starting transfers between devices  38.2 us (6%)
  between operations  14.1 us (2%)
  matrix products  7.75 us (1%)
    all_to_all x1, waiting for transfers between devices, per_device(): lax.all_to_all(fisher, 'mp', split_axis=2, concat_axis=0, tiled=True)  171 us
    unnamed x1, blocking collectives  166 us
    unnamed x16, local copies, waits for them, and re-layouts  72.4 us
    unnamed x2, other arithmetic  57.1 us
    all_gather x1, waiting for transfers between devices, per_device(): lax.all_gather(out_grads[0], 'shard', axis=0, tiled=True)  26.4 us
    reduce_sum x1, other arithmetic, merge_pair(): denominator = jnp.sum(fisher_float, axis=0)  25.3 us
    broadcast_in_dim x1, local copies, waits for them, and re-layouts, per_device(): fisher = (total / NSEQ).astype(jnp.bfloat16)[None]  18.7 us
    all_to_all x1, starting transfers between devices, per_device(): lax.all_to_all(fisher, 'mp', split_axis=2, concat_axis=0, tiled=True)  15.4 us
  transfers between devices with their start and end apart: 4, of which 2 were waited for; matrix products, arithmetic and copies ran while one was open for 24% of the time, Pallas kernels for 0%

commit v1 on v0

v1 whole, which is shorter than its diff:
```python
import functools

import jax
import jax.numpy as jnp
from jax import lax
from jax.experimental import pallas as pl
from jax.experimental.pallas import tpu as pltpu
from jax.sharding import PartitionSpec as P

MESH = pl.DeviceIdType.MESH
F32, BF16 = jnp.float32, jnp.bfloat16
RING = 4
TOK = 4
ROWS = 448
HALF = ROWS // 2
COLS = 256
WIDE = RING * COLS
PAIR = 2 * ROWS
ACT = PAIR + 128
TILE = 32
epsilon = 1e-6


def kernel(act_ref, grad_ref, own_ref, w_ref, out_ref,
           act_msg, act_in, act_pack, act_all,
           grad_msg, grad_in, grad_pack, grad_all,
           tmp_a, tmp_b, turned, lhs, wbuf,
           zsend, far_up, far_down, near_up, near_down,
           send_sems, recv_sems, w_sems, z_sems):
    mp, shard = lax.axis_index("mp"), lax.axis_index("shard")
    y, zh = mp // RING, lax.rem(mp, RING)
    x, zl, c = shard // (2 * RING), lax.rem(shard // 2, RING), lax.rem(shard, 2)

    def at(dy=0, dzh=0, dx=0, dzl=0, dc=0):
        yy, zz = lax.rem(y + dy, RING), lax.rem(zh + dzh, RING)
        xx, ll = lax.rem(x + dx, RING), lax.rem(zl + dzl, RING)
        cc = lax.rem(c + dc, 2)
        return (yy * RING + zz, (xx * RING + ll) * 2 + cc)

    hops = [(i, j) for i in range(RING) for j in range(RING)]
    partners = [at(dy=i, dzl=j) for i, j in hops if (i, j) != (0, 0)]
    partners += [at(dy=i, dx=j) for i, j in hops if j != 0]
    partners += [at(dc=1), at(dzh=1), at(dzh=3)]

    sends = []

    def push(src, dst, recv_sem, target):
        copy = pltpu.make_async_remote_copy(
            src_ref=src, dst_ref=dst, send_sem=send_sems.at[len(sends)],
            recv_sem=recv_sem, device_id=target, device_id_type=MESH)
        copy.start()
        sends.append(copy)

    def await_all(buf, sem):
        pltpu.make_async_copy(buf, buf, sem).wait()

    barrier = pltpu.get_barrier_semaphore()
    for target in partners:
        pl.semaphore_signal(barrier, inc=1, device_id=target, device_id_type=MESH)

    rows4 = lax.broadcasted_iota(jnp.int32, (TOK, 128), 0)
    owner = jnp.zeros((TOK, 128), F32)
    for t in range(TOK):
        owner = owner + jnp.where(rows4 == t, own_ref[0, t].astype(F32), 0.0)
    for l in range(RING):
        for i in range(RING):
            col = (i * RING + l) * PAIR
            tmp_a[l, TOK * i:TOK * (i + 1), :PAIR] = act_ref[0, :, col:col + PAIR].astype(F32)
            tmp_a[l, TOK * i:TOK * (i + 1), PAIR:] = owner
        act_msg[l] = tmp_a[l].astype(BF16)
    for i in range(RING):
        for q in range(RING):
            col = i * WIDE + q * COLS
            tmp_b[i, TOK * q:TOK * (q + 1), :COLS] = grad_ref[0, :, col:col + COLS].astype(F32)
        grad_msg[i] = tmp_b[i, :, :COLS].astype(BF16)

    pl.semaphore_wait(barrier, len(partners))

    for j in range(RING):
        to = lax.rem(zl + j, RING)
        if j == 0:
            pltpu.make_async_copy(act_msg.at[to], act_in.at[zl], recv_sems.at[0]).start()
        else:
            push(act_msg.at[to], act_in.at[zl], recv_sems.at[0], at(dzl=j))
    for i, j in hops:
        to = lax.rem(y + i, RING)
        if (i, j) == (0, 0):
            pltpu.make_async_copy(grad_msg.at[to], grad_in.at[y, zl], recv_sems.at[1]).start()
        else:
            push(grad_msg.at[to], grad_in.at[y, zl], recv_sems.at[1], at(dy=i, dzl=j))

    def send_weights(d):
        slot = d % RING
        block = lax.rem(zh + slot, RING)
        for i in range(RING):
            to = lax.rem(y + i, RING)
            cols = pl.ds(pl.multiple_of(to * WIDE + block * COLS, COLS), COLS)
            src, dst = w_ref.at[0, :, cols], wbuf.at[slot, y]
            if i == 0:
                pltpu.make_async_copy(src, dst, w_sems.at[slot]).start()
            else:
                push(src, dst, w_sems.at[slot], at(dy=i))

    send_weights(2)

    await_all(act_in, recv_sems.at[0])
    for l in range(RING):
        tmp_a[l] = act_in[l].astype(F32)
    for i in range(RING):
        for l in range(RING):
            tmp_b[i, TOK * l:TOK * (l + 1), :] = tmp_a[l, TOK * i:TOK * (i + 1), :]
        act_pack[i] = tmp_b[i].astype(BF16)
    for i, j in hops:
        to = lax.rem(x + j, RING)
        if (i, j) == (0, 0):
            pltpu.make_async_copy(act_pack.at[to], act_all.at[c, y, x], recv_sems.at[2]).start()
        else:
            push(act_pack.at[to], act_all.at[c, y, x], recv_sems.at[2], at(dy=i, dx=j))

    await_all(grad_in, recv_sems.at[1])
    for i in range(RING):
        for l in range(RING):
            tmp_a[l, :, :COLS] = grad_in[i, l].astype(F32)
        for l in range(RING):
            for q in range(RING):
                tmp_b[i, TOK * l:TOK * (l + 1), COLS * q:COLS * (q + 1)] = tmp_a[l, TOK * q:TOK * (q + 1), :COLS]
        grad_pack[i] = tmp_b[i].astype(BF16)
    for j in range(RING):
        if j == 0:
            pltpu.make_async_copy(grad_pack, grad_all.at[c, x], recv_sems.at[3]).start()
        else:
            push(grad_pack, grad_all.at[c, x], recv_sems.at[3], at(dx=j))

    send_weights(1)

    await_all(act_all.at[c], recv_sems.at[2])
    push(act_all.at[c], act_all.at[c], recv_sems.at[4], at(dc=1))
    await_all(grad_all.at[c], recv_sems.at[3])
    push(grad_all.at[c], grad_all.at[c], recv_sems.at[5], at(dc=1))

    send_weights(3)
    send_weights(0)

    other = 1 - c
    await_all(act_all.at[other], recv_sems.at[4])
    mine = pl.ds(pl.multiple_of(c * 384, 128), 512)
    for i in range(RING):
        own = act_all[:, i, :, :, PAIR:].reshape(128, 128).astype(F32).T[0:1, :]
        turned[...] = act_all[:, i, :, :, mine].reshape(128, 512).astype(F32).T
        units = turned[pl.ds(pl.multiple_of(c * 64, 64), ROWS), :]
        lhs[i, 0] = (units * (1.0 - own)).astype(BF16)
        lhs[i, 1] = (units * own).astype(BF16)
    await_all(grad_all.at[other], recv_sems.at[5])

    def partial_sums(d, start, stop, sink):
        slot = d % RING
        cols = pl.ds(pl.multiple_of(lax.rem(zh + slot, RING) * COLS, COLS), COLS)

        @pl.loop(start // TILE, stop // TILE)
        def _(step):
            rows = pl.ds(pl.multiple_of(step * TILE, TILE), TILE)
            num = jnp.zeros((TILE, COLS), F32)
            den = jnp.zeros((TILE, COLS), F32)
            for i in range(RING):
                grads = grad_all[:, :, i, :, cols].reshape(128, COLS)
                one = jnp.dot(lhs[i, 0, rows, :], grads, preferred_element_type=F32)
                two = jnp.dot(lhs[i, 1, rows, :], grads, preferred_element_type=F32)
                fisher = ((one * one + two * two) * 0.5).astype(BF16).astype(F32)
                num = num + fisher * wbuf[slot, i, rows, :].astype(F32)
                den = den + fisher
            sink(rows, num, den)

    def store(at_slot):
        def sink(rows, num, den):
            zsend[at_slot, 0, rows, :] = num.astype(BF16)
            zsend[at_slot, 1, rows, :] = den.astype(BF16)
        return sink

    def store_added(at_slot, got, offset):
        def sink(rows, num, den):
            there = pl.ds(pl.multiple_of(rows.start - offset, TILE), TILE)
            zsend[at_slot, 0, rows, :] = (num + got[0, there, :].astype(F32)).astype(BF16)
            zsend[at_slot, 1, rows, :] = (den + got[1, there, :].astype(F32)).astype(BF16)
        return sink

    top, bottom = pl.ds(0, HALF), pl.ds(HALF, HALF)
    await_all(wbuf.at[2], w_sems.at[2])
    partial_sums(2, 0, HALF, store(0))
    push(zsend.at[0, :, top], far_up, z_sems.at[0], at(dzh=1))
    partial_sums(2, HALF, ROWS, store(0))
    push(zsend.at[0, :, bottom], far_down, z_sems.at[1], at(dzh=3))
    await_all(wbuf.at[1], w_sems.at[1])
    partial_sums(1, HALF, ROWS, store(1))
    push(zsend.at[1, :, bottom], near_up.at[:, bottom], z_sems.at[2], at(dzh=1))
    await_all(wbuf.at[3], w_sems.at[3])
    partial_sums(3, 0, HALF, store(2))
    push(zsend.at[2, :, top], near_down.at[:, top], z_sems.at[3], at(dzh=3))

    await_all(far_up, z_sems.at[0])
    partial_sums(1, 0, HALF, store_added(1, far_up, 0))
    push(zsend.at[1, :, top], near_up.at[:, top], z_sems.at[4], at(dzh=1))
    await_all(far_down, z_sems.at[1])
    partial_sums(3, HALF, ROWS, store_added(2, far_down, HALF))
    push(zsend.at[2, :, bottom], near_down.at[:, bottom], z_sems.at[5], at(dzh=3))

    for copy in sends[:-6]:
        copy.wait_send()
    await_all(wbuf.at[0], w_sems.at[0])
    await_all(near_up.at[:, bottom], z_sems.at[2])
    await_all(near_down.at[:, top], z_sems.at[3])
    await_all(near_up.at[:, top], z_sems.at[4])
    await_all(near_down.at[:, bottom], z_sems.at[5])

    def finish(rows, num, den):
        num = num + (near_up[0, rows, :].astype(F32) + near_down[0, rows, :].astype(F32))
        den = den + (near_up[1, rows, :].astype(F32) + near_down[1, rows, :].astype(F32))
        out_ref[rows, :] = (num / (den + epsilon)).astype(BF16)

    partial_sums(0, 0, ROWS, finish)
    for copy in sends[-6:]:
        copy.wait_send()


def per_device(activations, out_grads, owners, weights):
    vmem = pl.BlockSpec(memory_space=pltpu.VMEM)
    return pl.pallas_call(
        kernel,
        out_shape=jax.ShapeDtypeStruct((ROWS, COLS), BF16),
        in_specs=[vmem, vmem, pl.BlockSpec(memory_space=pltpu.SMEM), pl.BlockSpec(memory_space=pl.ANY)],
        out_specs=vmem,
        scratch_shapes=[
            pltpu.VMEM((RING, 16, ACT), BF16),
            pltpu.VMEM((RING, 16, ACT), BF16),
            pltpu.VMEM((RING, 16, ACT), BF16),
            pltpu.VMEM((2, RING, RING, 16, ACT), BF16),
            pltpu.VMEM((RING, 16, COLS), BF16),
            pltpu.VMEM((RING, RING, 16, COLS), BF16),
            pltpu.VMEM((RING, 16, WIDE), BF16),
            pltpu.VMEM((2, RING, RING, 16, WIDE), BF16),
            pltpu.VMEM((RING, 16, ACT), F32),
            pltpu.VMEM((RING, 16, WIDE), F32),
            pltpu.VMEM((512, 128), F32),
            pltpu.VMEM((RING, 2, ROWS, 128), BF16),
            pltpu.VMEM((RING, RING, ROWS, COLS), BF16),
            pltpu.VMEM((3, 2, ROWS, COLS), BF16),
            pltpu.VMEM((2, HALF, COLS), BF16),
            pltpu.VMEM((2, HALF, COLS), BF16),
            pltpu.VMEM((2, ROWS, COLS), BF16),
            pltpu.VMEM((2, ROWS, COLS), BF16),
            pltpu.SemaphoreType.DMA((64,)),
            pltpu.SemaphoreType.DMA((6,)),
            pltpu.SemaphoreType.DMA((RING,)),
            pltpu.SemaphoreType.DMA((6,)),
        ],
        compiler_params=pltpu.CompilerParams(
            collective_id=0, has_side_effects=True, vmem_limit_bytes=56 << 20),
    )(activations, out_grads, owners, weights)


def solution(mesh):
    return jax.shard_map(
        per_device,
        mesh=mesh,
        in_specs=(
            P("mp", "shard", None),
            P("mp", "shard", None),
            P("mp", "shard"),
            P("mp", "shard", None),
        ),
        out_specs=P("shard", "mp"),
        check_vma=False,
    )
```

time: 603 us -> 111 us (0.18)
  the two profiles are of different devices: /device:TPU:121 before, /device:TPU:45 now
where the time goes in v1:
time: 111 us
  Pallas kernels  109 us (98%)
  local copies, waits for them, and re-layouts  1.64 us (1%)
    pallas_call x1, Pallas kernels, per_device(): pl.pallas_call(kernel, out_shape=jax.ShapeDtypeStruct((ROWS, COLS), BF16)...  109 us

profile of v1, /device:TPU:45, one launch (start us, length us, event | category | flops | bytes accessed | tf_op | source)
XLA Modules:
  0.0 110.8 jit_solution(6886013691068095789)
XLA Ops:
  0.0 109.2 %shard_map.46 = bf16[448,256]{1,0:T(8,128)(2,1)} custom-call(bf16[1,4,14336]{2,1,0:T(4,128)(2,1)} %act_ref.1, bf16[1,4,4096]{2,1,0:T(4,128)(2,1)} %grad_ref.1, s32[1,4]{1,0:T(1,128)} %own_ref.1, bf16[1,448,4096]{2,1,0:T(8,128)(2,1)} %w_ref.1), custom_call_target="tpu_custom_call" | custom-call | tf_op jit(solution)/shard_map/pallas_call | solution.py:226
  109.2 1.6 %copy.6 = bf16[448,256]{1,0:T(8,128)(2,1)} copy(bf16[448,256]{1,0:T(8,128)(2,1)} %shard_map.46) | data formatting | bytes 458752

commit v2 on v0

v2 whole, which is shorter than its diff:
```python
import jax
import jax.numpy as jnp
from jax import lax
from jax.experimental import pallas as pl
from jax.experimental.pallas import tpu as pltpu
from jax.sharding import PartitionSpec as P

MESH = pl.DeviceIdType.MESH
F32, BF16 = jnp.float32, jnp.bfloat16
RING = 4
TOK = 4
TOKENS = 128
ROWS = 448
HALF = ROWS // 2
COLS = 256
WIDE = RING * COLS
PAIR = 2 * ROWS
SIDE = 512
UNITS = ROWS + 16
CUT = 240
TILE = 32
epsilon = 1e-6


def kernel(act_ref, grad_ref, own_ref, w_ref, out_ref,
           act_msg, act_in, act_pack, act_all,
           grad_msg, grad_in, grad_pack, grad_all,
           tmp_a, tmp_b, turned, by_y, by_z, lhs, wbuf,
           zsend, far_up, far_down, near_up, near_down,
           num_own, den_own, den_send, den_in,
           send_sems, recv_sems, w_sems, z_sems):
    mp, shard = lax.axis_index("mp"), lax.axis_index("shard")
    y, zh = mp // RING, lax.rem(mp, RING)
    x, zl, c = shard // (2 * RING), lax.rem(shard // 2, RING), lax.rem(shard, 2)

    def at(dy=0, dzh=0, dx=0, dzl=0, dc=0):
        yy, zz = lax.rem(y + dy, RING), lax.rem(zh + dzh, RING)
        xx, ll = lax.rem(x + dx, RING), lax.rem(zl + dzl, RING)
        cc = lax.rem(c + dc, 2)
        return (yy * RING + zz, (xx * RING + ll) * 2 + cc)

    hops = [(i, j) for i in range(RING) for j in range(RING)]
    partners = [at(dy=i, dzl=j) for i, j in hops if (i, j) != (0, 0)]
    partners += [at(dzh=i, dzl=j) for i, j in hops if i != 0]
    partners += [at(dx=i, dc=j) for i in range(RING) for j in range(2) if (i, j) != (0, 0)]

    sends = []

    def push(src, dst, recv_sem, target):
        copy = pltpu.make_async_remote_copy(
            src_ref=src, dst_ref=dst, send_sem=send_sems.at[len(sends)],
            recv_sem=recv_sem, device_id=target, device_id_type=MESH)
        copy.start()
        sends.append(copy)

    def keep(src, dst, sem):
        pltpu.make_async_copy(src, dst, sem).start()

    def await_all(buf, sem):
        pltpu.make_async_copy(buf, buf, sem).wait()

    barrier = pltpu.get_barrier_semaphore()
    for target in partners:
        pl.semaphore_signal(barrier, inc=1, device_id=target, device_id_type=MESH)

    rows4 = lax.broadcasted_iota(jnp.int32, (TOK, 128), 0)
    low = lax.broadcasted_iota(jnp.int32, (TOK, 128), 1) < 64
    owner = jnp.zeros((TOK, 128), F32)
    for t in range(TOK):
        owner = owner + jnp.where(rows4 == t, own_ref[0, t].astype(F32), 0.0)
    for l in range(RING):
        for i in range(RING):
            col = (i * RING + l) * PAIR
            to = slice(TOK * i, TOK * (i + 1))
            middle = act_ref[0, :, col + 384:col + 512].astype(F32)
            tmp_a[l, to, 0:384] = act_ref[0, :, col:col + 384].astype(F32)
            tmp_a[l, to, 384:512] = jnp.where(low, middle, owner)
            tmp_a[l, to, 512:640] = jnp.where(low, owner, middle)
            tmp_a[l, to, 640:1024] = act_ref[0, :, col + 512:col + PAIR].astype(F32)
        act_msg[l] = tmp_a[l].astype(BF16)
    for g in range(2):
        for i in range(RING):
            for q in range(RING):
                col = i * WIDE + q * COLS if g == 0 else q * WIDE + i * COLS
                tmp_b[i, TOK * q:TOK * (q + 1), :COLS] = grad_ref[0, :, col:col + COLS].astype(F32)
            grad_msg[g, i] = tmp_b[i, :, :COLS].astype(BF16)

    pl.semaphore_wait(barrier, len(partners))

    def send_grads(g):
        ring = y if g == 0 else zh
        for i, j in hops:
            src, dst = grad_msg.at[g, lax.rem(ring + i, RING)], grad_in.at[g, ring, zl]
            if (i, j) == (0, 0):
                keep(src, dst, recv_sems.at[1 + g])
            else:
                push(src, dst, recv_sems.at[1 + g], at(dy=i, dzl=j) if g == 0 else at(dzh=i, dzl=j))

    def send_weights(d, part):
        slot, rows = d % RING, pl.ds(part * HALF, HALF)
        block = lax.rem(zh + slot, RING)
        for i in (2, 1, 3, 0):
            to = lax.rem(y + i, RING)
            cols = pl.ds(pl.multiple_of(to * WIDE + block * COLS, COLS), COLS)
            src, dst = w_ref.at[0, rows, cols], wbuf.at[slot, part, y]
            if i == 0:
                keep(src, dst, w_sems.at[2 * slot + part])
            else:
                push(src, dst, w_sems.at[2 * slot + part], at(dy=i))

    def await_weights(d, part):
        await_all(wbuf.at[d % RING, part], w_sems.at[2 * (d % RING) + part])

    for j in range(RING):
        src, dst = act_msg.at[lax.rem(zl + j, RING)], act_in.at[zl]
        if j == 0:
            keep(src, dst, recv_sems.at[0])
        else:
            push(src, dst, recv_sems.at[0], at(dzl=j))
    send_grads(0)
    send_weights(2, 0)
    send_weights(2, 1)

    await_all(act_in, recv_sems.at[0])
    for l in range(RING):
        tmp_a[l] = act_in[l].astype(F32)
    for i in range(RING):
        for l in range(RING):
            tmp_b[i, TOK * l:TOK * (l + 1), :] = tmp_a[l, TOK * i:TOK * (i + 1), :]
        for j in range(2):
            act_pack[j, i] = tmp_b[i, :, j * SIDE:(j + 1) * SIDE].astype(BF16)
    for i in range(RING):
        for j in range(2):
            src, dst = act_pack.at[lax.rem(c + j, 2), lax.rem(x + i, RING)], act_all.at[c, x]
            if (i, j) == (0, 0):
                keep(src, dst, recv_sems.at[3])
            else:
                push(src, dst, recv_sems.at[3], at(dx=i, dc=j))
    send_grads(1)

    def spread_grads(g):
        await_all(grad_in.at[g], recv_sems.at[1 + g])
        for i in range(RING):
            for l in range(RING):
                tmp_a[l, :, :COLS] = grad_in[g, i, l].astype(F32)
            for l in range(RING):
                for q in range(RING):
                    tmp_b[i, TOK * l:TOK * (l + 1), COLS * q:COLS * (q + 1)] = tmp_a[l, TOK * q:TOK * (q + 1), :COLS]
            grad_pack[g, i] = tmp_b[i].astype(BF16)
        for j in range(RING):
            if j == 0:
                keep(grad_pack.at[g], grad_all.at[g, c, x], recv_sems.at[4 + g])
            else:
                push(grad_pack.at[g], grad_all.at[g, c, x], recv_sems.at[4 + g], at(dx=j))

    spread_grads(0)

    await_all(act_all, recv_sems.at[3])
    turned[...] = act_all[...].reshape(TOKENS, SIDE).astype(F32).T
    by_z[0, :ROWS] = turned[pl.ds(pl.multiple_of(c * 64, 64), ROWS), :].astype(BF16)
    by_z[0, ROWS:] = turned[pl.ds(pl.multiple_of((1 - c) * ROWS, 64), 16), :].astype(BF16)
    keep(by_z.at[0], by_y.at[y], recv_sems.at[8])
    for i in (2, 1, 3):
        push(by_z.at[0], by_y.at[y], recv_sems.at[8], at(dy=i))
    push(by_z.at[0], by_z.at[3], recv_sems.at[9], at(dzh=1))
    push(by_z.at[0], by_z.at[1], recv_sems.at[10], at(dzh=3))
    send_weights(1, 1)
    send_weights(3, 0)
    spread_grads(1)

    def share_grads(g):
        await_all(grad_all.at[g, c], recv_sems.at[4 + g])
        push(grad_all.at[g, c], grad_all.at[g, c], recv_sems.at[6 + g], at(dc=1))

    def masked(g, i, units):
        one = units[ROWS:]
        body = units[:ROWS].reshape(ROWS // 16, 16, TOKENS)
        lhs[g, i, 0] = (body * (1 - one)[None]).reshape(ROWS, TOKENS)
        lhs[g, i, 1] = (body * one[None]).reshape(ROWS, TOKENS)

    share_grads(0)
    await_all(by_y, recv_sems.at[8])
    for i in range(RING):
        masked(0, i, by_y[i])
    await_all(grad_all.at[0, 1 - c], recv_sems.at[6])

    def fishers(g, block, rows):
        cols = pl.ds(pl.multiple_of(block * COLS, COLS), COLS)
        for i in range(RING):
            model = i if g == 0 else lax.rem(zh + i, RING)
            grads = grad_all[g, :, :, model, :, cols].reshape(TOKENS, COLS)
            one = jnp.dot(lhs[g, i, 0, rows, :], grads, preferred_element_type=F32)
            two = jnp.dot(lhs[g, i, 1, rows, :], grads, preferred_element_type=F32)
            yield ((one * one + two * two) * 0.5).astype(BF16).astype(F32)

    def numerators(d, part, sink):
        slot = d % RING

        @pl.loop(0, HALF // TILE, unroll=HALF // TILE)
        def _(step):
            there = pl.ds(pl.multiple_of(step * TILE, TILE), TILE)
            rows = pl.ds(pl.multiple_of(part * HALF + step * TILE, TILE), TILE)
            num = jnp.zeros((TILE, COLS), F32)
            for i, fisher in enumerate(fishers(0, lax.rem(zh + slot, RING), rows)):
                num = num + fisher * wbuf[slot, part, i, there, :].astype(F32)
            sink(rows, there, num)

    def store(slot, got=None):
        def sink(rows, there, num):
            if got is not None:
                num = num + got[there, :].astype(F32)
            zsend[slot, rows, :] = num.astype(BF16)
        return sink

    top, bottom = pl.ds(0, HALF), pl.ds(HALF, HALF)
    await_weights(2, 0)
    numerators(2, 0, store(0))
    push(zsend.at[0, top], far_up, z_sems.at[0], at(dzh=1))
    await_weights(2, 1)
    numerators(2, 1, store(0))
    push(zsend.at[0, bottom], far_down, z_sems.at[1], at(dzh=3))
    send_weights(1, 0)
    send_weights(3, 1)
    share_grads(1)
    await_weights(1, 1)
    numerators(1, 1, store(1))
    push(zsend.at[1, bottom], near_up.at[bottom], z_sems.at[2], at(dzh=1))
    await_weights(3, 0)
    numerators(3, 0, store(2))
    push(zsend.at[2, top], near_down.at[top], z_sems.at[3], at(dzh=3))
    send_weights(0, 0)
    send_weights(0, 1)

    await_all(by_z.at[3], recv_sems.at[9])
    push(by_z.at[3, :CUT], by_z.at[2, :CUT], recv_sems.at[11], at(dzh=1))
    await_all(by_z.at[1], recv_sems.at[10])
    push(by_z.at[1, CUT:], by_z.at[2, CUT:], recv_sems.at[12], at(dzh=3))

    await_all(far_up, z_sems.at[0])
    await_weights(1, 0)
    numerators(1, 0, store(1, far_up))
    push(zsend.at[1, top], near_up.at[top], z_sems.at[4], at(dzh=1))
    await_all(far_down, z_sems.at[1])
    await_weights(3, 1)
    numerators(3, 1, store(2, far_down))
    push(zsend.at[2, bottom], near_down.at[bottom], z_sems.at[5], at(dzh=3))

    await_all(grad_all.at[1, 1 - c], recv_sems.at[7])
    for i in (0, 1, 3):
        masked(1, i, by_z[i])
    await_all(by_z.at[2, :CUT], recv_sems.at[11])
    await_all(by_z.at[2, CUT:], recv_sems.at[12])
    masked(1, 2, by_z[2])
    for i in (2, 1, 3, 0):
        @pl.loop(0, ROWS // TILE, unroll=HALF // TILE)
        def _(step, i=i):
            rows = pl.ds(pl.multiple_of(step * TILE, TILE), TILE)
            den = jnp.zeros((TILE, COLS), F32)
            for fisher in fishers(1, lax.rem(y + i, RING), rows):
                den = den + fisher
            if i == 0:
                den_own[rows, :] = den
            else:
                den_send[i - 1, rows, :] = den.astype(BF16)
        if i != 0:
            push(den_send.at[i - 1], den_in.at[i - 1], recv_sems.at[13], at(dy=i))

    for part in range(2):
        def hold(rows, there, num):
            num_own[rows, :] = num
        await_weights(0, part)
        numerators(0, part, hold)

    for copy in sends[:-5]:
        copy.wait_send()
    await_all(den_in, recv_sems.at[13])
    await_all(near_up.at[bottom], z_sems.at[2])
    await_all(near_down.at[top], z_sems.at[3])
    await_all(near_up.at[top], z_sems.at[4])
    await_all(near_down.at[bottom], z_sems.at[5])

    @pl.loop(0, ROWS // TILE, unroll=HALF // TILE)
    def _(step):
        rows = pl.ds(pl.multiple_of(step * TILE, TILE), TILE)
        num = num_own[rows, :] + (near_up[rows, :].astype(F32) + near_down[rows, :].astype(F32))
        den = den_own[rows, :]
        for i in range(RING - 1):
            den = den + den_in[i, rows, :].astype(F32)
        out_ref[rows, :] = (num / (den + epsilon)).astype(BF16)

    for copy in sends[-5:]:
        copy.wait_send()


def per_device(activations, out_grads, owners, weights):
    vmem = pl.BlockSpec(memory_space=pltpu.VMEM)
    return pl.pallas_call(
        kernel,
        out_shape=jax.ShapeDtypeStruct((ROWS, COLS), BF16),
        in_specs=[vmem, vmem, pl.BlockSpec(memory_space=pltpu.SMEM), pl.BlockSpec(memory_space=pl.ANY)],
        out_specs=vmem,
        scratch_shapes=[
            pltpu.VMEM((RING, 16, 2 * SIDE), BF16),
            pltpu.VMEM((RING, 16, 2 * SIDE), BF16),
            pltpu.VMEM((2, RING, 16, SIDE), BF16),
            pltpu.VMEM((2, RING, 16, SIDE), BF16),
            pltpu.VMEM((2, RING, 16, COLS), BF16),
            pltpu.VMEM((2, RING, RING, 16, COLS), BF16),
            pltpu.VMEM((2, RING, 16, WIDE), BF16),
            pltpu.VMEM((2, 2, RING, RING, 16, WIDE), BF16),
            pltpu.VMEM((RING, 16, WIDE), F32),
            pltpu.VMEM((RING, 16, WIDE), F32),
            pltpu.VMEM((SIDE, TOKENS), F32),
            pltpu.VMEM((RING, UNITS, TOKENS), BF16),
            pltpu.VMEM((RING, UNITS, TOKENS), BF16),
            pltpu.VMEM((2, RING, 2, ROWS, TOKENS), BF16),
            pltpu.VMEM((RING, 2, RING, HALF, COLS), BF16),
            pltpu.VMEM((3, ROWS, COLS), BF16),
            pltpu.VMEM((HALF, COLS), BF16),
            pltpu.VMEM((HALF, COLS), BF16),
            pltpu.VMEM((ROWS, COLS), BF16),
            pltpu.VMEM((ROWS, COLS), BF16),
            pltpu.VMEM((ROWS, COLS), F32),
            pltpu.VMEM((ROWS, COLS), F32),
            pltpu.VMEM((3, ROWS, COLS), BF16),
            pltpu.VMEM((3, ROWS, COLS), BF16),
            pltpu.SemaphoreType.DMA((96,)),
            pltpu.SemaphoreType.DMA((14,)),
            pltpu.SemaphoreType.DMA((2 * RING,)),
            pltpu.SemaphoreType.DMA((6,)),
        ],
        compiler_params=pltpu.CompilerParams(
            collective_id=0, has_side_effects=True, vmem_limit_bytes=56 << 20),
    )(activations, out_grads, owners, weights)


def solution(mesh):
    return jax.shard_map(
        per_device,
        mesh=mesh,
        in_specs=(
            P("mp", "shard", None),
            P("mp", "shard", None),
            P("mp", "shard"),
            P("mp", "shard", None),
        ),
        out_specs=P("shard", "mp"),
        check_vma=False,
    )
```

time: 603 us -> 93.4 us (0.15)
  the two profiles are of different devices: /device:TPU:121 before, /device:TPU:1 now
where the time goes in v2:
time: 93.4 us; the launch traced here: 93.3 us
  Pallas kernels  91.6 us (98%)
  local copies, waits for them, and re-layouts  1.64 us (2%)
    pallas_call x1, Pallas kernels, per_device(): pl.pallas_call(kernel, out_shape=jax.ShapeDtypeStruct((ROWS, COLS), BF16)...  91.6 us

profile of v2, /device:TPU:1, one launch (start us, length us, event | category | flops | bytes accessed | tf_op | source)
XLA Modules:
  0.0 93.3 jit_solution(4396283163425447192)
XLA Ops:
  0.0 91.6 %shard_map.46 = bf16[448,256]{1,0:T(8,128)(2,1)} custom-call(bf16[1,4,14336]{2,1,0:T(4,128)(2,1)} %act_ref.1, bf16[1,4,4096]{2,1,0:T(4,128)(2,1)} %grad_ref.1, s32[1,4]{1,0:T(1,128)} %own_ref.1, bf16[1,448,4096]{2,1,0:T(8,128)(2,1)} %w_ref.1), custom_call_target="tpu_custom_call" | custom-call | tf_op jit(solution)/shard_map/pallas_call | solution.py:297
  91.6 1.6 %copy.6 = bf16[448,256]{1,0:T(8,128)(2,1)} copy(bf16[448,256]{1,0:T(8,128)(2,1)} %shard_map.46) | data formatting | bytes 458752

commit v3 on v2

v3 whole, which is shorter than its diff:
```python
import jax
import jax.numpy as jnp
from jax import lax
from jax.experimental import pallas as pl
from jax.experimental.pallas import tpu as pltpu
from jax.sharding import PartitionSpec as P

MESH = pl.DeviceIdType.MESH
F32, BF16 = jnp.float32, jnp.bfloat16
RING = 4
TOK = 4
TOKENS = 128
ROWS = 448
HALF = ROWS // 2
COLS = 256
WIDE = RING * COLS
PAIR = 2 * ROWS
SIDE = 512
UNITS = ROWS + 16
CUT = 240
TILE = 32
epsilon = 1e-6


def kernel(act_hbm, grad_hbm, own_ref, w_ref, out_ref,
           act_ref, grad_ref,
           act_msg, act_in, act_pack, act_all,
           grad_msg, grad_in, grad_pack, grad_all,
           tmp_a, tmp_b, turned, by_y, by_z, lhs, wbuf, wown,
           ring_send, far_in, near_in, num_own, den_own,
           send_sems, recv_sems, w_sems, own_sems, ring_sems, grad_sems):
    mp, shard = lax.axis_index("mp"), lax.axis_index("shard")
    y, zh = mp // RING, lax.rem(mp, RING)
    x, zl, c = shard // (2 * RING), lax.rem(shard // 2, RING), lax.rem(shard, 2)

    def at(dy=0, dzh=0, dx=0, dzl=0, dc=0):
        yy, zz = lax.rem(y + dy, RING), lax.rem(zh + dzh, RING)
        xx, ll = lax.rem(x + dx, RING), lax.rem(zl + dzl, RING)
        cc = lax.rem(c + dc, 2)
        return (yy * RING + zz, (xx * RING + ll) * 2 + cc)

    hops = [(i, j) for i in range(RING) for j in range(RING)]
    partners = [at(dy=i, dzl=j) for i, j in hops if (i, j) != (0, 0)]
    partners += [at(dzh=i, dzl=j) for i, j in hops if i != 0]
    partners += [at(dx=i, dc=j) for i in range(RING) for j in range(2) if (i, j) != (0, 0)]

    sends = []

    def push(src, dst, recv_sem, target):
        copy = pltpu.make_async_remote_copy(
            src_ref=src, dst_ref=dst, send_sem=send_sems.at[len(sends)],
            recv_sem=recv_sem, device_id=target, device_id_type=MESH)
        copy.start()
        sends.append(copy)

    def keep(src, dst, sem):
        pltpu.make_async_copy(src, dst, sem).start()

    def await_all(buf, sem):
        pltpu.make_async_copy(buf, buf, sem).wait()

    inputs = (pltpu.make_async_copy(act_hbm, act_ref, recv_sems.at[4]),
              pltpu.make_async_copy(grad_hbm, grad_ref, recv_sems.at[5]))
    for copy in inputs:
        copy.start()
    barrier = pltpu.get_barrier_semaphore()
    for target in partners:
        pl.semaphore_signal(barrier, inc=1, device_id=target, device_id_type=MESH)

    rows4 = lax.broadcasted_iota(jnp.int32, (TOK, 128), 0)
    low = lax.broadcasted_iota(jnp.int32, (TOK, 128), 1) < 64
    owner = jnp.zeros((TOK, 128), F32)
    for t in range(TOK):
        owner = owner + jnp.where(rows4 == t, own_ref[0, t].astype(F32), 0.0)
    for copy in inputs:
        copy.wait()
    for l in range(RING):
        for i in range(RING):
            col = (i * RING + l) * PAIR
            to = slice(TOK * i, TOK * (i + 1))
            middle = act_ref[0, :, col + 384:col + 512].astype(F32)
            tmp_a[l, to, 0:384] = act_ref[0, :, col:col + 384].astype(F32)
            tmp_a[l, to, 384:512] = jnp.where(low, middle, owner)
            tmp_a[l, to, 512:640] = jnp.where(low, owner, middle)
            tmp_a[l, to, 640:1024] = act_ref[0, :, col + 512:col + PAIR].astype(F32)
        act_msg[l] = tmp_a[l].astype(BF16)
    for g in range(2):
        for i in range(RING):
            for q in range(RING):
                col = i * WIDE + q * COLS if g == 0 else q * WIDE + i * COLS
                tmp_b[i, TOK * q:TOK * (q + 1), :COLS] = grad_ref[0, :, col:col + COLS].astype(F32)
            grad_msg[g, i] = tmp_b[i, :, :COLS].astype(BF16)

    pl.semaphore_wait(barrier, len(partners))

    def send_grads(g):
        ring = y if g == 0 else zh
        for i, j in hops:
            src, dst = grad_msg.at[g, lax.rem(ring + i, RING)], grad_in.at[g, ring, zl]
            if (i, j) == (0, 0):
                keep(src, dst, recv_sems.at[1 + g])
            else:
                push(src, dst, recv_sems.at[1 + g], at(dy=i, dzl=j) if g == 0 else at(dzh=i, dzl=j))

    def send_weights(d, part):
        slot, rows = d % RING, pl.ds(part * HALF, HALF)
        block = lax.rem(zh + slot, RING)
        for i in (2, 1, 3, 0):
            to = lax.rem(y + i, RING)
            cols = pl.ds(pl.multiple_of(to * WIDE + block * COLS, COLS), COLS)
            src, dst = w_ref.at[0, rows, cols], wbuf.at[slot - 1, part, y]
            if i == 0:
                keep(src, dst, w_sems.at[2 * slot + part])
            else:
                push(src, dst, w_sems.at[2 * slot + part], at(dy=i))

    def await_weights(d, part):
        await_all(wbuf.at[d - 1, part], w_sems.at[2 * d + part])

    for j in range(RING):
        src, dst = act_msg.at[lax.rem(zl + j, RING)], act_in.at[zl]
        if j == 0:
            keep(src, dst, recv_sems.at[0])
        else:
            push(src, dst, recv_sems.at[0], at(dzl=j))
    send_weights(2, 0)
    send_weights(2, 1)

    await_all(act_in, recv_sems.at[0])
    for l in range(RING):
        tmp_a[l] = act_in[l].astype(F32)
    for i in range(RING):
        for l in range(RING):
            tmp_b[i, TOK * l:TOK * (l + 1), :] = tmp_a[l, TOK * i:TOK * (i + 1), :]
        for j in range(2):
            act_pack[j, i] = tmp_b[i, :, j * SIDE:(j + 1) * SIDE].astype(BF16)
    for i in range(RING):
        for j in range(2):
            src, dst = act_pack.at[lax.rem(c + j, 2), lax.rem(x + i, RING)], act_all.at[c, x]
            if (i, j) == (0, 0):
                keep(src, dst, recv_sems.at[3])
            else:
                push(src, dst, recv_sems.at[3], at(dx=i, dc=j))
    send_grads(0)

    def pack_grads(g):
        await_all(grad_in.at[g], recv_sems.at[1 + g])
        for i in range(RING):
            for l in range(RING):
                tmp_a[l, :, :COLS] = grad_in[g, i, l].astype(F32)
            for l in range(RING):
                for q in range(RING):
                    tmp_b[i, TOK * l:TOK * (l + 1), COLS * q:COLS * (q + 1)] = tmp_a[l, TOK * q:TOK * (q + 1), :COLS]
            grad_pack[g, i] = tmp_b[i].astype(BF16)

    def grad_block(g, k):
        return pl.ds(pl.multiple_of(lax.rem((y if g else zh) + k, RING) * COLS, COLS), COLS)

    def spread_grads(g, k):
        src = grad_pack.at[g, :, :, grad_block(g, k)]
        dst = grad_all.at[g, c, x, :, :, grad_block(g, k)]
        keep(src, dst, grad_sems.at[g, 0, k])
        for i in (2, 1, 3):
            push(src, dst, grad_sems.at[g, 0, k], at(dx=i))

    def share_grads(g, k):
        both = grad_all.at[g, c, :, :, :, grad_block(g, k)]
        await_all(both, grad_sems.at[g, 0, k])
        push(both, both, grad_sems.at[g, 1, k], at(dc=1))

    def await_grads(g, k):
        await_all(grad_all.at[g, 1 - c, :, :, :, grad_block(g, k)], grad_sems.at[g, 1, k])

    await_all(act_all, recv_sems.at[3])
    turned[...] = act_all[...].reshape(TOKENS, SIDE).astype(F32).T
    by_z[0, :ROWS] = turned[pl.ds(pl.multiple_of(c * 64, 64), ROWS), :].astype(BF16)
    by_z[0, ROWS:] = turned[pl.ds(pl.multiple_of((1 - c) * ROWS, 64), 16), :].astype(BF16)
    keep(by_z.at[0], by_y.at[y], recv_sems.at[8])
    for i in (2, 1, 3):
        push(by_z.at[0], by_y.at[y], recv_sems.at[8], at(dy=i))
    push(by_z.at[0], by_z.at[3], recv_sems.at[9], at(dzh=1))
    push(by_z.at[0], by_z.at[1], recv_sems.at[10], at(dzh=3))
    pack_grads(0)
    for k in (2, 1, 3):
        spread_grads(0, k)
    send_weights(1, 1)
    send_weights(3, 0)
    send_grads(1)
    for i in (2, 1, 3, 0):
        cols = lax.rem(y + i, RING) * WIDE + zh * COLS
        keep(w_ref.at[0, :, pl.ds(pl.multiple_of(cols, COLS), COLS)], wown.at[i], own_sems.at[i])

    def masked(g, i, units):
        one = units[ROWS:]
        body = units[:ROWS].reshape(ROWS // 16, 16, TOKENS)
        lhs[g, i, 0] = (body * (1 - one)[None]).reshape(ROWS, TOKENS)
        lhs[g, i, 1] = (body * one[None]).reshape(ROWS, TOKENS)

    share_grads(0, 2)
    await_all(by_y, recv_sems.at[8])
    for i in range(RING):
        masked(0, i, by_y[i])
    await_grads(0, 2)

    def fishers(g, block, rows, models=RING):
        cols = pl.ds(pl.multiple_of(block * COLS, COLS), COLS)
        for i in range(models):
            model = i if g == 0 else lax.rem(zh + i, RING)
            grads = grad_all[g, :, :, model, :, cols].reshape(TOKENS, COLS)
            one = jnp.dot(lhs[g, i, 0, rows, :], grads, preferred_element_type=F32)
            two = jnp.dot(lhs[g, i, 1, rows, :], grads, preferred_element_type=F32)
            yield ((one * one + two * two) * 0.5).astype(BF16).astype(F32)

    def over_rows(part, body):
        @pl.loop(0, HALF // TILE, unroll=HALF // TILE)
        def _(step):
            there = pl.ds(pl.multiple_of(step * TILE, TILE), TILE)
            rows = pl.ds(pl.multiple_of(part * HALF + step * TILE, TILE), TILE)
            body(rows, there)

    def y_ring_numerators(d, part, rows, there):
        num = jnp.zeros((TILE, COLS), F32)
        for i, fisher in enumerate(fishers(0, lax.rem(zh + d, RING), rows)):
            num = num + fisher * wbuf[d - 1, part, i, there, :].astype(F32)
        return num

    def own_numerators(d, part, rows, there):
        for fisher in fishers(1, lax.rem(y + d, RING), rows, 1):
            return fisher * wown[d, rows, :].astype(F32)

    def denominators(d, part, rows, there):
        den = jnp.zeros((TILE, COLS), F32)
        for fisher in fishers(1, lax.rem(y + d, RING), rows):
            den = den + fisher
        return den

    terms = (y_ring_numerators, own_numerators, denominators)

    def step_to(r, d):
        return at(dzh=d) if r == 0 else at(dy=d)

    def give(r, d, part, got=None):
        slot = d - 1

        def body(rows, there):
            value = terms[r](d, part, rows, there)
            if got is not None:
                value = value + got[there, :].astype(F32)
            ring_send[r, slot, rows, :] = value.astype(BF16)
        over_rows(part, body)
        src = ring_send.at[r, slot, pl.ds(part * HALF, HALF)]
        if d == 2:
            push(src, far_in.at[r, part], ring_sems.at[r, part], step_to(r, 1 if part == 0 else 3))
        else:
            side = 0 if d == 1 else 1
            push(src, near_in.at[r, side, part], ring_sems.at[r, 2 + 2 * side + part], step_to(r, d))

    def give_added(r, d):
        part = 0 if d == 1 else 1
        await_all(far_in.at[r, part], ring_sems.at[r, part])
        give(r, d, part, far_in.at[r, part])

    def received(r, part, there):
        return near_in[r, 0, part, there, :].astype(F32) + near_in[r, 1, part, there, :].astype(F32)

    await_weights(2, 0)
    give(0, 2, 0)
    await_weights(2, 1)
    give(0, 2, 1)
    send_weights(1, 0)
    send_weights(3, 1)
    share_grads(0, 1)
    share_grads(0, 3)
    pack_grads(1)
    for k in (2, 1, 3, 0):
        spread_grads(1, k)

    await_all(by_z.at[3], recv_sems.at[9])
    push(by_z.at[3, :CUT], by_z.at[2, :CUT], recv_sems.at[11], at(dzh=1))
    await_all(by_z.at[1], recv_sems.at[10])
    push(by_z.at[1, CUT:], by_z.at[2, CUT:], recv_sems.at[12], at(dzh=3))

    for k in (2, 1, 3, 0):
        share_grads(1, k)
    await_weights(1, 1)
    await_grads(0, 1)
    give(0, 1, 1)
    await_weights(3, 0)
    await_grads(0, 3)
    give(0, 3, 0)
    for i in (0, 1, 3):
        masked(1, i, by_z[i])
    for i in (2, 1, 3, 0):
        await_all(wown.at[i], own_sems.at[i])
    await_grads(1, 2)
    give(1, 2, 0)
    give(1, 2, 1)
    await_grads(1, 1)
    give(1, 1, 1)
    await_grads(1, 3)
    give(1, 3, 0)
    await_all(by_z.at[2, :CUT], recv_sems.at[11])
    await_all(by_z.at[2, CUT:], recv_sems.at[12])
    masked(1, 2, by_z[2])
    give(2, 2, 0)
    give(2, 2, 1)
    give(2, 1, 1)
    give(2, 3, 0)
    await_weights(1, 0)
    give_added(0, 1)
    await_weights(3, 1)
    give_added(0, 3)
    give_added(1, 1)
    give_added(1, 3)
    await_grads(1, 0)
    for part in range(2):
        def hold(rows, there, part=part):
            num_own[rows, :] = own_numerators(0, part, rows, there)
            den_own[rows, :] = denominators(0, part, rows, there)
        over_rows(part, hold)
    give_added(2, 1)
    give_added(2, 3)

    for copy in sends[:-5]:
        copy.wait_send()
    for part in range(2):
        for r in range(3):
            for side in range(2):
                await_all(near_in.at[r, side, part], ring_sems.at[r, 2 + 2 * side + part])

        def finish(rows, there, part=part):
            num = num_own[rows, :] + (received(0, part, there) + received(1, part, there))
            den = den_own[rows, :] + received(2, part, there)
            out_ref[rows, :] = (num / (den + epsilon)).astype(BF16)
        over_rows(part, finish)

    for copy in sends[-5:]:
        copy.wait_send()


def per_device(activations, out_grads, owners, weights):
    hbm, vmem = pl.BlockSpec(memory_space=pl.ANY), pl.BlockSpec(memory_space=pltpu.VMEM)
    return pl.pallas_call(
        kernel,
        out_shape=jax.ShapeDtypeStruct((ROWS, COLS), BF16),
        in_specs=[hbm, hbm, pl.BlockSpec(memory_space=pltpu.SMEM), hbm],
        out_specs=vmem,
        scratch_shapes=[
            pltpu.VMEM(activations.shape, BF16),
            pltpu.VMEM(out_grads.shape, BF16),
            pltpu.VMEM((RING, 16, 2 * SIDE), BF16),
            pltpu.VMEM((RING, 16, 2 * SIDE), BF16),
            pltpu.VMEM((2, RING, 16, SIDE), BF16),
            pltpu.VMEM((2, RING, 16, SIDE), BF16),
            pltpu.VMEM((2, RING, 16, COLS), BF16),
            pltpu.VMEM((2, RING, RING, 16, COLS), BF16),
            pltpu.VMEM((2, RING, 16, WIDE), BF16),
            pltpu.VMEM((2, 2, RING, RING, 16, WIDE), BF16),
            pltpu.VMEM((RING, 16, WIDE), F32),
            pltpu.VMEM((RING, 16, WIDE), F32),
            pltpu.VMEM((SIDE, TOKENS), F32),
            pltpu.VMEM((RING, UNITS, TOKENS), BF16),
            pltpu.VMEM((RING, UNITS, TOKENS), BF16),
            pltpu.VMEM((2, RING, 2, ROWS, TOKENS), BF16),
            pltpu.VMEM((RING - 1, 2, RING, HALF, COLS), BF16),
            pltpu.VMEM((RING, ROWS, COLS), BF16),
            pltpu.VMEM((3, 3, ROWS, COLS), BF16),
            pltpu.VMEM((3, 2, HALF, COLS), BF16),
            pltpu.VMEM((3, 2, 2, HALF, COLS), BF16),
            pltpu.VMEM((ROWS, COLS), F32),
            pltpu.VMEM((ROWS, COLS), F32),
            pltpu.SemaphoreType.DMA((128,)),
            pltpu.SemaphoreType.DMA((14,)),
            pltpu.SemaphoreType.DMA((2 * RING,)),
            pltpu.SemaphoreType.DMA((RING,)),
            pltpu.SemaphoreType.DMA((3, 6)),
            pltpu.SemaphoreType.DMA((2, 2, RING)),
        ],
        compiler_params=pltpu.CompilerParams(
            collective_id=0, has_side_effects=True, vmem_limit_bytes=56 << 20),
    )(activations, out_grads, owners, weights)


def solution(mesh):
    return jax.shard_map(
        per_device,
        mesh=mesh,
        in_specs=(
            P("mp", "shard", None),
            P("mp", "shard", None),
            P("mp", "shard"),
            P("mp", "shard", None),
        ),
        out_specs=P("shard", "mp"),
        check_vma=False,
    )
```

time: 93.4 us -> 84 us (0.90)
  the two profiles are of different devices: /device:TPU:1 before, /device:TPU:89 now
where the time goes in v3:
time: 84 us; the launch traced here: 83.8 us
  Pallas kernels  82.2 us (98%)
  local copies, waits for them, and re-layouts  1.64 us (2%)
    pallas_call x1, Pallas kernels, per_device(): pl.pallas_call(kernel, out_shape=jax.ShapeDtypeStruct((ROWS, COLS), BF16)...  82.2 us

profile of v3, /device:TPU:89, one launch (start us, length us, event | category | flops | bytes accessed | tf_op | source)
XLA Modules:
  0.0 83.8 jit_solution(5456535914700100865)
XLA Ops:
  0.0 82.2 %shard_map.46 = bf16[448,256]{1,0:T(8,128)(2,1)} custom-call(bf16[1,4,14336]{2,1,0:T(4,128)(2,1)} %act_hbm.1, bf16[1,4,4096]{2,1,0:T(4,128)(2,1)} %grad_hbm.1, s32[1,4]{1,0:T(1,128)} %own_ref.1, bf16[1,448,4096]{2,1,0:T(8,128)(2,1)} %w_ref.1), custom_call_target="tpu_custom_call" | custom-call | tf_op jit(solution)/shard_map/pallas_call | solution.py:343
  82.2 1.6 %copy.6 = bf16[448,256]{1,0:T(8,128)(2,1)} copy(bf16[448,256]{1,0:T(8,128)(2,1)} %shard_map.46) | data formatting | bytes 458752

commit v4 on v3

--- a/solution.py
+++ b/solution.py
@@ -18,14 +18,14 @@
 SIDE = 512
 UNITS = ROWS + 16
 CUT = 240
-TILE = 32
+TILE = 112
 epsilon = 1e-6
 
 
 def kernel(act_hbm, grad_hbm, own_ref, w_ref, out_ref,
            act_ref, grad_ref,
            act_msg, act_in, act_pack, act_all,
-           grad_msg, grad_in, grad_pack, grad_all,
+           grad_msg, grad_step, grad_in, grad_pack, grad_all,
            tmp_a, tmp_b, turned, by_y, by_z, lhs, wbuf, wown,
            ring_send, far_in, near_in, num_own, den_own,
            send_sems, recv_sems, w_sems, own_sems, ring_sems, grad_sems):
@@ -39,9 +39,8 @@
         cc = lax.rem(c + dc, 2)
         return (yy * RING + zz, (xx * RING + ll) * 2 + cc)
 
-    hops = [(i, j) for i in range(RING) for j in range(RING)]
-    partners = [at(dy=i, dzl=j) for i, j in hops if (i, j) != (0, 0)]
-    partners += [at(dzh=i, dzl=j) for i, j in hops if i != 0]
+    partners = [at(dy=i) for i in range(1, RING)] + [at(dzl=i) for i in range(1, RING)]
+    partners += [at(dzh=i) for i in range(1, RING)]
     partners += [at(dx=i, dc=j) for i in range(RING) for j in range(2) if (i, j) != (0, 0)]
 
     sends = []
@@ -72,8 +71,7 @@
     owner = jnp.zeros((TOK, 128), F32)
     for t in range(TOK):
         owner = owner + jnp.where(rows4 == t, own_ref[0, t].astype(F32), 0.0)
-    for copy in inputs:
-        copy.wait()
+    inputs[0].wait()
     for l in range(RING):
         for i in range(RING):
             col = (i * RING + l) * PAIR
@@ -84,23 +82,25 @@
             tmp_a[l, to, 512:640] = jnp.where(low, owner, middle)
             tmp_a[l, to, 640:1024] = act_ref[0, :, col + 512:col + PAIR].astype(F32)
         act_msg[l] = tmp_a[l].astype(BF16)
-    for g in range(2):
+    pl.semaphore_wait(barrier, len(partners))
+
+    def send_grads(g):
+        ring = zh if g else y
         for i in range(RING):
-            for q in range(RING):
-                col = i * WIDE + q * COLS if g == 0 else q * WIDE + i * COLS
-                tmp_b[i, TOK * q:TOK * (q + 1), :COLS] = grad_ref[0, :, col:col + COLS].astype(F32)
-            grad_msg[g, i] = tmp_b[i, :, :COLS].astype(BF16)
-
-    pl.semaphore_wait(barrier, len(partners))
-
-    def send_grads(g):
-        ring = y if g == 0 else zh
-        for i, j in hops:
-            src, dst = grad_msg.at[g, lax.rem(ring + i, RING)], grad_in.at[g, ring, zl]
-            if (i, j) == (0, 0):
+            src, dst = grad_msg.at[g, lax.rem(ring + i, RING)], grad_step.at[g, ring]
+            if i == 0:
+                keep(src, dst, recv_sems.at[6 + g])
+            else:
+                push(src, dst, recv_sems.at[6 + g], at(dzh=i) if g else at(dy=i))
+
+    def send_grads_on(g):
+        await_all(grad_step.at[g], recv_sems.at[6 + g])
+        for j in range(RING):
+            src, dst = grad_step.at[g], grad_in.at[g, :, zl]
+            if j == 0:
                 keep(src, dst, recv_sems.at[1 + g])
             else:
-                push(src, dst, recv_sems.at[1 + g], at(dy=i, dzl=j) if g == 0 else at(dzh=i, dzl=j))
+                push(src, dst, recv_sems.at[1 + g], at(dzl=j))
 
     def send_weights(d, part):
         slot, rows = d % RING, pl.ds(part * HALF, HALF)
@@ -123,6 +123,15 @@
             keep(src, dst, recv_sems.at[0])
         else:
             push(src, dst, recv_sems.at[0], at(dzl=j))
+    inputs[1].wait()
+    for g in range(2):
+        for i in range(RING):
+            for q in range(RING):
+                col = i * WIDE + q * COLS if g == 0 else q * WIDE + i * COLS
+                tmp_b[i, TOK * q:TOK * (q + 1), :COLS] = grad_ref[0, :, col:col + COLS].astype(F32)
+            grad_msg[g, i] = tmp_b[i, :, :COLS].astype(BF16)
+    send_grads(0)
+    send_grads(1)
     send_weights(2, 0)
     send_weights(2, 1)
 
@@ -141,7 +150,7 @@
                 keep(src, dst, recv_sems.at[3])
             else:
                 push(src, dst, recv_sems.at[3], at(dx=i, dc=j))
-    send_grads(0)
+    send_grads_on(0)
 
     def pack_grads(g):
         await_all(grad_in.at[g], recv_sems.at[1 + g])
@@ -175,17 +184,17 @@
     turned[...] = act_all[...].reshape(TOKENS, SIDE).astype(F32).T
     by_z[0, :ROWS] = turned[pl.ds(pl.multiple_of(c * 64, 64), ROWS), :].astype(BF16)
     by_z[0, ROWS:] = turned[pl.ds(pl.multiple_of((1 - c) * ROWS, 64), 16), :].astype(BF16)
-    keep(by_z.at[0], by_y.at[y], recv_sems.at[8])
+    push(by_z.at[0], by_z.at[3], recv_sems.at[9], at(dzh=1))
+    push(by_z.at[0], by_z.at[1], recv_sems.at[10], at(dzh=3))
     for i in (2, 1, 3):
         push(by_z.at[0], by_y.at[y], recv_sems.at[8], at(dy=i))
-    push(by_z.at[0], by_z.at[3], recv_sems.at[9], at(dzh=1))
-    push(by_z.at[0], by_z.at[1], recv_sems.at[10], at(dzh=3))
+    keep(by_z.at[0], by_y.at[y], recv_sems.at[8])
     pack_grads(0)
     for k in (2, 1, 3):
         spread_grads(0, k)
     send_weights(1, 1)
     send_weights(3, 0)
-    send_grads(1)
+    send_grads_on(1)
     for i in (2, 1, 3, 0):
         cols = lax.rem(y + i, RING) * WIDE + zh * COLS
         keep(w_ref.at[0, :, pl.ds(pl.multiple_of(cols, COLS), COLS)], wown.at[i], own_sems.at[i])
@@ -212,7 +221,7 @@
             yield ((one * one + two * two) * 0.5).astype(BF16).astype(F32)
 
     def over_rows(part, body):
-        @pl.loop(0, HALF // TILE, unroll=HALF // TILE)
+        @pl.loop(0, HALF // TILE, unroll=1)
         def _(step):
             there = pl.ds(pl.multiple_of(step * TILE, TILE), TILE)
             rows = pl.ds(pl.multiple_of(part * HALF + step * TILE, TILE), TILE)
@@ -323,15 +332,23 @@
 
     for copy in sends[:-5]:
         copy.wait_send()
+    def arrived(r, part):
+        for side in range(2):
+            await_all(near_in.at[r, side, part], ring_sems.at[r, 2 + 2 * side + part])
+
     for part in range(2):
-        for r in range(3):
-            for side in range(2):
-                await_all(near_in.at[r, side, part], ring_sems.at[r, 2 + 2 * side + part])
+        arrived(1, part)
+        arrived(2, part)
+
+        def combine(rows, there, part=part):
+            num_own[rows, :] = num_own[rows, :] + received(1, part, there)
+            den_own[rows, :] = 1.0 / (den_own[rows, :] + received(2, part, there) + epsilon)
+        over_rows(part, combine)
+    for part in range(2):
+        arrived(0, part)
 
         def finish(rows, there, part=part):
-            num = num_own[rows, :] + (received(0, part, there) + received(1, part, there))
-            den = den_own[rows, :] + received(2, part, there)
-            out_ref[rows, :] = (num / (den + epsilon)).astype(BF16)
+            out_ref[rows, :] = ((num_own[rows, :] + received(0, part, there)) * den_own[rows, :]).astype(BF16)
         over_rows(part, finish)
 
     for copy in sends[-5:]:
@@ -352,6 +369,7 @@
             pltpu.VMEM((RING, 16, 2 * SIDE), BF16),
             pltpu.VMEM((2, RING, 16, SIDE), BF16),
             pltpu.VMEM((2, RING, 16, SIDE), BF16),
+            pltpu.VMEM((2, RING, 16, COLS), BF16),
             pltpu.VMEM((2, RING, 16, COLS), BF16),
             pltpu.VMEM((2, RING, RING, 16, COLS), BF16),
             pltpu.VMEM((2, RING, 16, WIDE), BF16),

time: 84 us -> 81.4 us (0.969)
  the two profiles are of different devices: /device:TPU:89 before, /device:TPU:96 now
where the time goes in v4:
time: 81.4 us; the launch traced here: 81.2 us
  Pallas kernels  79.5 us (98%)
  local copies, waits for them, and re-layouts  1.64 us (2%)
    pallas_call x1, Pallas kernels, per_device(): pl.pallas_call(kernel, out_shape=jax.ShapeDtypeStruct((ROWS, COLS), BF16)...  79.5 us
    unnamed x1, local copies, waits for them, and re-layouts  1.64 us

profile of v4, /device:TPU:96, one launch (start us, length us, event | category | flops | bytes accessed | tf_op | source)
XLA Modules:
  0.0 81.2 jit_solution(17177299675609767148)
XLA Ops:
  0.0 79.5 %shard_map.46 = bf16[448,256]{1,0:T(8,128)(2,1)} custom-call(bf16[1,4,14336]{2,1,0:T(4,128)(2,1)} %act_hbm.1, bf16[1,4,4096]{2,1,0:T(4,128)(2,1)} %grad_hbm.1, s32[1,4]{1,0:T(1,128)} %own_ref.1, bf16[1,448,4096]{2,1,0:T(8,128)(2,1)} %w_ref.1), custom_call_target="tpu_custom_call" | custom-call | tf_op jit(solution)/shard_map/pallas_call | solution.py:360
  79.5 1.6 %copy.6 = bf16[448,256]{1,0:T(8,128)(2,1)} copy(bf16[448,256]{1,0:T(8,128)(2,1)} %shard_map.46) | data formatting | bytes 458752

commit v5 on v4

--- a/solution.py
+++ b/solution.py
@@ -22,8 +22,7 @@
 epsilon = 1e-6
 
 
-def kernel(act_hbm, grad_hbm, own_ref, w_ref, out_ref,
-           act_ref, grad_ref,
+def kernel(act_ref, grad_ref, own_ref, w_ref, out_ref,
            act_msg, act_in, act_pack, act_all,
            grad_msg, grad_step, grad_in, grad_pack, grad_all,
            tmp_a, tmp_b, turned, by_y, by_z, lhs, wbuf, wown,
@@ -58,10 +57,6 @@
     def await_all(buf, sem):
         pltpu.make_async_copy(buf, buf, sem).wait()
 
-    inputs = (pltpu.make_async_copy(act_hbm, act_ref, recv_sems.at[4]),
-              pltpu.make_async_copy(grad_hbm, grad_ref, recv_sems.at[5]))
-    for copy in inputs:
-        copy.start()
     barrier = pltpu.get_barrier_semaphore()
     for target in partners:
         pl.semaphore_signal(barrier, inc=1, device_id=target, device_id_type=MESH)
@@ -71,7 +66,6 @@
     owner = jnp.zeros((TOK, 128), F32)
     for t in range(TOK):
         owner = owner + jnp.where(rows4 == t, own_ref[0, t].astype(F32), 0.0)
-    inputs[0].wait()
     for l in range(RING):
         for i in range(RING):
             col = (i * RING + l) * PAIR
@@ -123,7 +117,6 @@
             keep(src, dst, recv_sems.at[0])
         else:
             push(src, dst, recv_sems.at[0], at(dzl=j))
-    inputs[1].wait()
     for g in range(2):
         for i in range(RING):
             for q in range(RING):
@@ -192,8 +185,6 @@
     pack_grads(0)
     for k in (2, 1, 3):
         spread_grads(0, k)
-    send_weights(1, 1)
-    send_weights(3, 0)
     send_grads_on(1)
     for i in (2, 1, 3, 0):
         cols = lax.rem(y + i, RING) * WIDE + zh * COLS
@@ -207,6 +198,8 @@
 
     share_grads(0, 2)
     await_all(by_y, recv_sems.at[8])
+    send_weights(1, 1)
+    send_weights(3, 0)
     for i in range(RING):
         masked(0, i, by_y[i])
     await_grads(0, 2)
@@ -330,7 +323,7 @@
     give_added(2, 1)
     give_added(2, 3)
 
-    for copy in sends[:-5]:
+    for copy in sends[:-6]:
         copy.wait_send()
     def arrived(r, part):
         for side in range(2):
@@ -351,7 +344,7 @@
             out_ref[rows, :] = ((num_own[rows, :] + received(0, part, there)) * den_own[rows, :]).astype(BF16)
         over_rows(part, finish)
 
-    for copy in sends[-5:]:
+    for copy in sends[-6:]:
         copy.wait_send()
 
 
@@ -360,11 +353,9 @@
     return pl.pallas_call(
         kernel,
         out_shape=jax.ShapeDtypeStruct((ROWS, COLS), BF16),
-        in_specs=[hbm, hbm, pl.BlockSpec(memory_space=pltpu.SMEM), hbm],
+        in_specs=[vmem, vmem, pl.BlockSpec(memory_space=pltpu.SMEM), hbm],
         out_specs=vmem,
         scratch_shapes=[
-            pltpu.VMEM(activations.shape, BF16),
-            pltpu.VMEM(out_grads.shape, BF16),
             pltpu.VMEM((RING, 16, 2 * SIDE), BF16),
             pltpu.VMEM((RING, 16, 2 * SIDE), BF16),
             pltpu.VMEM((2, RING, 16, SIDE), BF16),

time: 81.4 us -> 80.9 us (level)
  the two profiles are of different devices: /device:TPU:96 before, /device:TPU:89 now
where the time goes in v5:
time: 80.9 us; the launch traced here: 79.7 us
  Pallas kernels  78.1 us (97%)
  local copies, waits for them, and re-layouts  1.64 us (2%)
    pallas_call x1, Pallas kernels, per_device(): pl.pallas_call(kernel, out_shape=jax.ShapeDtypeStruct((ROWS, COLS), BF16)...  78.1 us
    unnamed x1, local copies, waits for them, and re-layouts  1.64 us

profile of v5, /device:TPU:89, one launch (start us, length us, event | category | flops | bytes accessed | tf_op | source)
XLA Modules:
  0.0 79.7 jit_solution(2737138606018396754)
XLA Ops:
  0.0 78.1 %shard_map.46 = bf16[448,256]{1,0:T(8,128)(2,1)} custom-call(bf16[1,4,14336]{2,1,0:T(4,128)(2,1)} %act_ref.1, bf16[1,4,4096]{2,1,0:T(4,128)(2,1)} %grad_ref.1, s32[1,4]{1,0:T(1,128)} %own_ref.1, bf16[1,448,4096]{2,1,0:T(8,128)(2,1)} %w_ref.1), custom_call_target="tpu_custom_call" | custom-call | tf_op jit(solution)/shard_map/pallas_call | solution.py:353
  78.1 1.6 %copy.6 = bf16[448,256]{1,0:T(8,128)(2,1)} copy(bf16[448,256]{1,0:T(8,128)(2,1)} %shard_map.46) | data formatting | bytes 458752
